TPU v7x, 32 devices: a whole 2x2x4 slice. The times are simulated.
32 devices in a mesh: tile: 8 (over z, y), member: 4 (over x, core).
Axes of the slice: x: 2, y: 2, z: 4, core: 2. Of those that a mesh axis runs over, the one named last changes fastest.
Arguments:
- latent: float32 [4, 4, 64, 8192], P('member', None, None, 'tile'), may hold values from -6 to 6
- noise: float32 [4, 4, 64, 8192], P('member', None, None, 'tile'), may hold values from -6 to 6
- features: bfloat16 [64, 64, 8192], P('member', None, 'tile'), may hold values from -6 to 6
- slot_window: int32 [48], P('tile'), may hold values from -1 to 254, as said below
- timestep: int32 [1], replicated, may hold values from 200 to 999
- time_weight: bfloat16 [64, 64], replicated, may hold values from -0.75 to 0.75
- in_weight: bfloat16 [64, 36], replicated, may hold values from -1 to 1
- conv1_weight: bfloat16 [64, 576], replicated, may hold values from -0.25 to 0.25
- conv2_weight: bfloat16 [64, 576], replicated, may hold values from -0.25 to 0.25
- out_weight: bfloat16 [4, 576], replicated, may hold values from -0.25 to 0.25
- norm1_gain: float32 [64], replicated, may hold values from 0.1 to 1.9
- norm2_gain: float32 [64], replicated, may hold values from 0.1 to 1.9
- norm3_gain: float32 [64], replicated, may hold values from 0.1 to 1.9
Outputs:
- latent_prev: float32 [4, 4, 64, 8192], P('member', None, None, 'tile')
Inputs may be any that keep to these rules, and one draw needn't show every extreme that they name: `slot_window`: entry j of tile t's 6 slots (index t * 6 + j) is -1 for an empty slot or a window whose columns all lie in tiles t - 1 to t + 1; a window may be listed in several slots, and each listing counts.
All inputs are finite; a program needn't handle non-finite values.
Results may differ from a plain program's by a relative error of at most 0.0003.
Values may be sent and summed in bfloat16 or wider, within the bound.
A program may use at most 128 MiB of HBM per device.

v0:
```python
import math
import jax
import jax.numpy as jnp
from jax import lax
from jax.sharding import PartitionSpec as P

LAT = 4
WIN = 64
REACH = 1
TRAIN_STEPS = 1000
STRIDE = 20
GROUPS = 32
norm_epsilon = 1e-05
eta_noise = 0.5
beta_first = 0.00085
beta_last = 0.012


def with_halo(block, sides, width):
    for axis, dim in sides:
        count = lax.axis_size(axis)
        forward = [(i, i + 1) for i in range(count - 1)]
        backward = [(target, source) for source, target in forward]
        low = lax.ppermute(
            lax.slice_in_dim(block, block.shape[dim] - width, None, axis=dim), axis, forward
        )
        high = lax.ppermute(lax.slice_in_dim(block, 0, width, axis=dim), axis, backward)
        block = jnp.concatenate([low, block, high], axis=dim)
    return block


def from_behind(value, axis, by):
    length = lax.axis_size(axis)
    pairs = [(i, i + by) for i in range(length) if 0 <= i + by < length]
    return lax.ppermute(value, axis, pairs)


def plan_terms(timestep):
    betas_root = jnp.linspace(beta_first**0.5, beta_last**0.5, TRAIN_STEPS, dtype=jnp.float32)
    kept = 1.0 - betas_root * betas_root
    step = jnp.arange(TRAIN_STEPS, dtype=jnp.int32)
    current = jnp.prod(jnp.where(step <= timestep[0], kept, 1.0))
    earlier = jnp.prod(jnp.where(step <= timestep[0] - STRIDE, kept, 1.0))
    sigma_sq = eta_noise * eta_noise * (1.0 - earlier) / (1.0 - current) * (1.0 - current / earlier)
    return (current, earlier, sigma_sq)


def time_embed(timestep, time_weight):
    half_width = time_weight.shape[0] // 2
    freqs_row = jnp.exp(-math.log(10000.0) * jnp.arange(half_width, dtype=jnp.float32) / half_width)
    angles = timestep[0].astype(jnp.float32) * freqs_row
    embedding = jnp.concatenate([jnp.cos(angles), jnp.sin(angles)]).astype(jnp.bfloat16)
    return jax.nn.silu(
        jnp.dot(embedding[None, :], time_weight, preferred_element_type=jnp.float32)[0]
    )


def conv_same(activation, weight, window_side):
    cell_count = activation.shape[-1]
    column = jnp.arange(cell_count, dtype=jnp.int32) % window_side
    padded = jnp.pad(activation, ((0, 0), (window_side + 1, window_side + 1)))
    tap_list = []
    for row_shift in (-1, 0, 1):
        for col_shift in (-1, 0, 1):
            anchor = window_side + 1 + row_shift * window_side + col_shift
            tap_piece = padded[:, anchor : anchor + cell_count]
            if col_shift == -1:
                tap_piece = jnp.where(column >= 1, tap_piece, jnp.zeros_like(tap_piece))
            if col_shift == 1:
                tap_piece = jnp.where(
                    column <= window_side - 2, tap_piece, jnp.zeros_like(tap_piece)
                )
            tap_list.append(tap_piece)
    stacked = jnp.concatenate(tap_list, axis=0)
    return jnp.dot(weight, stacked, preferred_element_type=jnp.float32)


def group_norm(hidden, gain):
    channels, cell_count = hidden.shape
    grouped = hidden.reshape(GROUPS, channels // GROUPS * cell_count)
    center = jnp.mean(grouped, axis=1, keepdims=True)
    deviate = grouped - center
    spread_sq = jnp.mean(deviate * deviate, axis=1, keepdims=True)
    normed = (deviate * lax.rsqrt(spread_sq + norm_epsilon)).reshape(channels, cell_count)
    return normed * gain[:, None]


def denoiser(latent_win, feature_win, time_bias, weight_set):
    in_weight, conv1_weight, conv2_weight, out_weight, gain_one, gain_two, gain_three = weight_set
    hidden = conv_same(latent_win, in_weight, WIN) + feature_win.astype(jnp.float32)
    first_act = jax.nn.silu(group_norm(hidden, gain_one)).astype(jnp.bfloat16)
    middle = conv_same(first_act, conv1_weight, WIN) + time_bias[:, None]
    second_act = jax.nn.silu(group_norm(middle, gain_two)).astype(jnp.bfloat16)
    block_out = hidden + conv_same(second_act, conv2_weight, WIN)
    third_act = jax.nn.silu(group_norm(block_out, gain_three)).astype(jnp.bfloat16)
    return conv_same(third_act, out_weight, WIN)


def denoise_update(state_now, eps_mean, noise_draw, current, earlier, sigma_sq):
    clean_est = (state_now - jnp.sqrt(1.0 - current) * eps_mean) / jnp.sqrt(current)
    return (
        jnp.sqrt(earlier) * clean_est
        + jnp.sqrt(1.0 - earlier - sigma_sq) * eps_mean
        + jnp.sqrt(sigma_sq) * noise_draw
    )


def body(
    latent,
    noise,
    features,
    slot_window,
    timestep,
    time_weight,
    in_weight,
    conv1_weight,
    conv2_weight,
    out_weight,
    norm1_gain,
    norm2_gain,
    norm3_gain,
):
    tile_width = latent.shape[-1]
    half_win = WIN // 2
    rim_width = REACH * tile_width
    ext_width = tile_width + 2 * rim_width
    tile_index = lax.axis_index("tile")
    all_channels = lax.all_gather(features, "member", axis=0, tiled=True)
    driver_ext = with_halo(all_channels, (("tile", 2),), rim_width)
    latent_ext = with_halo(latent[0].astype(jnp.bfloat16), (("tile", 2),), rim_width)
    current, earlier, sigma_sq = plan_terms(timestep)
    time_bias = time_embed(timestep, time_weight)
    weight_set = (
        in_weight,
        conv1_weight,
        conv2_weight,
        out_weight,
        norm1_gain,
        norm2_gain,
        norm3_gain,
    )
    listed = slot_window >= 0
    listed_weight = listed.astype(jnp.float32)
    local_start = jnp.where(
        listed, slot_window * half_win - tile_index * tile_width + rim_width, rim_width
    )
    channels = driver_ext.shape[0]

    def one_slot(start_col):
        latent_win = lax.dynamic_slice_in_dim(latent_ext, start_col, WIN, 2).reshape(LAT, WIN * WIN)
        feature_win = lax.dynamic_slice_in_dim(driver_ext, start_col, WIN, 2).reshape(
            channels, WIN * WIN
        )
        return denoiser(latent_win, feature_win, time_bias, weight_set)

    eps_slots = lax.map(one_slot, local_start)

    def add_slot(running, packed):
        start_col, eps_window, weight_one = packed
        current_slab = lax.dynamic_slice_in_dim(running, start_col, WIN, 2)
        updated = current_slab + weight_one * eps_window.reshape(LAT, WIN, WIN)
        return (lax.dynamic_update_slice_in_dim(running, updated, start_col, 2), None)

    partial_ext, ignored = lax.scan(
        add_slot,
        jnp.zeros((LAT, WIN, ext_width), jnp.float32),
        (local_start, eps_slots, listed_weight),
    )
    ext_cols = jnp.arange(ext_width, dtype=jnp.int32)
    inside = (ext_cols[None, :] >= local_start[:, None]) & (
        ext_cols[None, :] < local_start[:, None] + WIN
    )
    cover_ext = jnp.sum(listed_weight[:, None] * inside.astype(jnp.float32), axis=0)
    eps_total = partial_ext[:, :, rim_width : rim_width + tile_width]
    cover_total = cover_ext[rim_width : rim_width + tile_width]
    distance = 1
    low_col = rim_width + distance * tile_width
    sums_piece = partial_ext[:, :, low_col : low_col + tile_width]
    count_piece = cover_ext[low_col : low_col + tile_width]
    got_sums = from_behind(sums_piece.astype(jnp.bfloat16), "tile", distance).astype(
        sums_piece.dtype
    )
    got_count = from_behind(count_piece.astype(jnp.bfloat16), "tile", distance).astype(
        count_piece.dtype
    )
    eps_total = eps_total + got_sums
    cover_total = cover_total + got_count
    distance = 1
    high_col = rim_width - (distance - 1) * tile_width
    low_col = high_col - tile_width
    sums_piece = partial_ext[:, :, low_col:high_col]
    count_piece = cover_ext[low_col:high_col]
    got_sums = from_behind(sums_piece.astype(jnp.bfloat16), "tile", -distance).astype(
        sums_piece.dtype
    )
    got_count = from_behind(count_piece.astype(jnp.bfloat16), "tile", -distance).astype(
        count_piece.dtype
    )
    eps_total = eps_total + got_sums
    cover_total = cover_total + got_count
    eps_mean = eps_total / jnp.maximum(cover_total, 1.0)[None, None, :]
    return denoise_update(latent[0], eps_mean, noise[0], current, earlier, sigma_sq)[None]


def solution(mesh):
    placed = (
        P("member", None, None, "tile"),
        P("member", None, None, "tile"),
        P("member", None, "tile"),
        P("tile"),
        P(),
        P(),
        P(),
        P(),
        P(),
        P(),
        P(),
        P(),
        P(),
    )
    return jax.shard_map(
        body, mesh=mesh, in_specs=placed, out_specs=P("member", None, None, "tile"), check_vma=False
    )
```

profile of v0, /device:TPU:9, one launch (start us, length us, event | category | flops | bytes accessed | tf_op | source)
XLA Modules:
  0.0 678.4 jit_solution(9812453653305107138)
XLA Ops:
  6.5 0.7 all-gather.2.cloned.1.call-update
  7.3 61.6 %all-gather.2.cloned.1.call-done = bf16[64,64,1024]{2,1,0:T(8,128)(2,1)} async-done(((bf16[16,64,1024]{2,1,0:T(8,128)(2,1)}), bf16[64,64,1024]{2,1,0:T(8,128)(2,1)}) %all-gather.2.cloned.1.call-update) | async-done | bytes 8388624 | tf_op jit(solution)/shard_map/all_gather | solution.py:128
  68.8 3.1 collective-permute-start.2
  71.9 3.1 collective-permute-start.3
  75.0 1.3 bitcast_convert_fusion
  76.3 2.2 collective-permute-start
  78.5 5.1 collective-permute-start.1
  86.0 368.0 %collective-permute-done = bf16[4,64,1024]{2,1,0:T(8,128)(2,1)S(1)} collective-permute-done((bf16[4,64,1024]{2,1,0:T(8,128)(2,1)S(1)}, bf16[4,64,1024]{2,1,0:T(8,128)(2,1)S(1)}, u32[]{:S(2)}, u32[]{:S(2)}) %collective-permute-start) | collective-permute-done | bytes 524320 | tf_op jit(solution)/shard_map/ppermute | solution.py:24
  454.0 2.5 collective-permute-done.1
  456.6 17.6 %pad_maximum_fusion = bf16[64,64,3072]{2,1,0:T(8,128)(2,1)} fusion(bf16[64,64,1024]{2,1,0:T(8,128)(2,1)} %collective-permute-done.3, bf16[64,64,1024]{2,1,0:T(8,128)(2,1)} %all-gather.2.cloned.1.call-done, bf16[64,64,1024]{2,1,0:T(8,128)(2,1)} %collective-permute-done.2), kind=kLoop, calls=%fused_computation.70 | loop fusion | flops 75497472 | bytes 50331648 | tf_op jit(solution)/shard_map/concatenate | solution.py:28
  474.2 127.3 %while.22 = (s32[]{:T(128)}, f32[6,4,4096]{2,1,0:T(4,128)}, s32[6]{0:T(128)S(1)}, bf16[4,64,3072]{2,1,0:T(8,128)(2,1)S(1)}, bf16[64,36]{0,1:T(8,128)(2,1)S(1)}, ...) while((s32[]{:T(128)}, f32[6,4,4096]{2,1,0:T(4,128)}, ...), condition=%wide.region_15.16_spmd, body=%wide.region_2.15_spmd.sunk | while | flops 663355456 | bytes 75635800 | solution.py:156
  474.3 0.8 dynamic_slice.46
  477.5 1.6 dynamic-slice_convert_fusion.2
  484.0 1.1 fusion.64
  488.9 1.1 fusion.66
  493.8 1.4 fusion.67
  495.2 0.7 dynamic_slice.46
  498.4 2.0 dynamic-slice_convert_fusion.2
  505.2 1.1 fusion.64
  510.2 1.1 fusion.66
  515.1 1.4 fusion.67
  516.5 0.7 dynamic_slice.46
  519.6 2.0 dynamic-slice_convert_fusion.2
  526.5 1.1 fusion.64
  531.5 1.1 fusion.66
  536.4 1.4 fusion.67
  537.8 0.7 dynamic_slice.46
  540.9 2.0 dynamic-slice_convert_fusion.2
  547.8 1.1 fusion.64
  552.7 1.1 fusion.66
  557.7 1.4 fusion.67
  559.0 0.7 dynamic_slice.46
  562.2 2.0 dynamic-slice_convert_fusion.2
  569.1 1.1 fusion.64
  574.0 1.1 fusion.66
  579.0 1.4 fusion.67
  580.3 0.7 dynamic_slice.46
  583.5 2.0 dynamic-slice_convert_fusion.2
  590.4 1.1 fusion.64
  595.3 1.1 fusion.66
  600.2 1.4 fusion.67
  601.9 36.7 %while.23 = (s32[]{:T(128)}, f32[4,64,3072]{2,1,0:T(8,128)S(1)}, s32[6]{0:T(128)S(1)}, f32[6]{0:T(128)S(1)}, f32[6,4,4096]{2,1,0:T(4,128)}, /*index=5*/s32[]{:T(128)}, s32[]{:T(128)}, s32[]{:T(128)}) while((s32[]{:T(128)}, f32[4,64,3072]{2,1,0:T(8,128)S(1)}, s32[6]{0:T(128)S(1)}, f32[6]{0:T(128)S(1)}, f32[6,4,4096]{2,1,0:T(4,128)}, ...), condition=%wide.region_17.18_spmd, body=%wide.region_16.17_spmd.sunk | while | flops 32773 | bytes 589983 | solution.py:164
  604.7 0.7 dynamic_slice.49
  605.4 1.5 dynamic-slice_multiply_fusion.2
  607.2 1.0 dynamic_update_slice.14
  610.9 0.7 dynamic_slice.49
  611.6 1.5 dynamic-slice_multiply_fusion.2
  616.6 0.7 dynamic_slice.49
  617.3 1.5 dynamic-slice_multiply_fusion.2
  619.1 1.1 dynamic_update_slice.14
  623.6 1.5 dynamic-slice_multiply_fusion.2
  625.4 1.1 dynamic_update_slice.14
  630.0 1.5 dynamic-slice_multiply_fusion.2
  631.8 1.1 dynamic_update_slice.14
  636.3 1.5 dynamic-slice_multiply_fusion.2
  638.8 1.0 fusion.29
  639.9 1.9 collective-permute-start.4
  641.8 4.3 collective-permute-start.5
  646.1 1.9 collective-permute-start.6
  648.0 4.2 collective-permute-start.7
  652.3 0.8 select_reduce_fusion.1
  657.1 7.4 %collective-permute-done.6 = bf16[1024]{0:T(1024)(128)(2,1)S(1)} collective-permute-done((bf16[1024]{0:T(1024)(128)(2,1)S(1)}, bf16[1024]{0:T(1024)(128)(2,1)S(1)}, u32[]{:S(2)}, u32[]{:S(2)}) %collective-permute-start.6) | collective-permute-done | bytes 2080 | tf_op jit(solution)/shard_map/ppermute | solution.py:35
  664.5 3.7 collective-permute-done.7
  668.2 3.3 fusion.12
  (523 shorter events, 87.6 us)
Async XLA Ops:
  6.5 79.2 %copy-start = (bf16[64,64]{1,0:T(8,128)(2,1)S(1)}, bf16[64,64]{1,0:T(8,128)(2,1)}, u32[]{:S(2)}) copy-start(bf16[64,64]{1,0:T(8,128)(2,1)} %param.22) | copy-start | bytes 24580
  6.5 62.3 %all-gather.2.cloned.1.call-start = ((), (), s32[]{:S(2)}) async-start(), calls=%async_computation | async-start | bytes 10485760 | tf_op jit(solution)/shard_map/all_gather | solution.py:128
  68.8 387.8 %collective-permute-start.2 = (bf16[64,64,1024]{2,1,0:T(8,128)(2,1)}, bf16[64,64,1024]{2,1,0:T(8,128)(2,1)}, u32[]{:S(2)}, u32[]{:S(2)}) collective-permute-start(bf16[64,64,1024]{2,1,0:T(8,128)(2,1)} %all-gather.2.cloned.1.call-done), channel_id=1, source_target_pairs={{0,4},{4,8},{8,12},{12,16},{16,20},{20,24},{24,28},{1,5},{5,9},{9,... | collective-permute-start | bytes 25165832 | tf_op jit(solution)/shard_map/ppermute | solution.py:24
  71.9 384.7 %collective-permute-start.3 = (bf16[64,64,1024]{2,1,0:T(8,128)(2,1)}, bf16[64,64,1024]{2,1,0:T(8,128)(2,1)}, u32[]{:S(2)}, u32[]{:S(2)}) collective-permute-start(bf16[64,64,1024]{2,1,0:T(8,128)(2,1)} %all-gather.2.cloned.1.call-done), channel_id=1, source_target_pairs={{4,0},{8,4},{12,8},{16,12},{20,16},{24,20},{28,24},{5,1},{9,5},{13... | collective-permute-start | bytes 25165832 | tf_op jit(solution)/shard_map/ppermute | solution.py:27
  76.3 377.6 %collective-permute-start = (bf16[4,64,1024]{2,1,0:T(8,128)(2,1)S(1)}, bf16[4,64,1024]{2,1,0:T(8,128)(2,1)S(1)}, u32[]{:S(2)}, u32[]{:S(2)}) collective-permute-start(bf16[4,64,1024]{2,1,0:T(8,128)(2,1)S(1)} %bitcast_convert_fusion), channel_id=1, source_target_pairs={{0,4},{4,8},{8,12},{12,16},{16,20},{20,24},{24,28},{1,5},{5,9},{9,... | collective-permute-start | bytes 1572872 | tf_op jit(solution)/shard_map/ppermute | solution.py:24
  78.5 377.9 %collective-permute-start.1 = (bf16[4,64,1024]{2,1,0:T(8,128)(2,1)S(1)}, bf16[4,64,1024]{2,1,0:T(8,128)(2,1)S(1)}, u32[]{:S(2)}, u32[]{:S(2)}) collective-permute-start(bf16[4,64,1024]{2,1,0:T(8,128)(2,1)S(1)} %bitcast_convert_fusion), channel_id=1, source_target_pairs={{4,0},{8,4},{12,8},{16,12},{20,16},{24,20},{28,24},{5,1},{9,5},{13... | collective-permute-start | bytes 1572872 | tf_op jit(solution)/shard_map/ppermute | solution.py:27
  456.5 17.7 %copy-start.6 = (bf16[64,36]{0,1:T(8,128)(2,1)S(1)}, bf16[64,36]{0,1:T(8,128)(2,1)}, u32[]{:S(2)}) copy-start(bf16[64,36]{0,1:T(8,128)(2,1)} %param.23) | copy-start | bytes 13828
  456.6 17.7 %copy-start.7 = (bf16[4,576]{1,0:T(4,128)(2,1)S(1)}, bf16[4,576]{1,0:T(4,128)(2,1)}, u32[]{:S(2)}) copy-start(bf16[4,576]{1,0:T(4,128)(2,1)} %param.26) | copy-start | bytes 13828
  456.6 17.7 %copy-start.8 = (f32[64]{0:T(128)S(1)}, f32[64]{0:T(128)}, u32[]{:S(2)}) copy-start(f32[64]{0:T(128)} %param.27) | copy-start | bytes 772
  456.6 17.7 %copy-start.9 = (f32[64]{0:T(128)S(1)}, f32[64]{0:T(128)}, u32[]{:S(2)}) copy-start(f32[64]{0:T(128)} %param.28) | copy-start | bytes 772
  456.6 17.7 %copy-start.10 = (f32[64]{0:T(128)S(1)}, f32[64]{0:T(128)}, u32[]{:S(2)}) copy-start(f32[64]{0:T(128)} %param.29) | copy-start | bytes 772
  474.3 2.7 copy-start.2
  482.0 2.0 copy-start.4
  486.9 2.0 copy-start.5
  492.9 2.3 copy-start.3
  495.2 2.7 copy-start.2
  503.3 2.0 copy-start.4
  508.2 2.0 copy-start.5
  514.2 2.3 copy-start.3
  516.5 2.7 copy-start.2
  524.5 2.0 copy-start.4
  529.5 2.0 copy-start.5
  535.5 2.3 copy-start.3
  537.8 2.7 copy-start.2
  545.8 2.0 copy-start.4
  550.8 2.0 copy-start.5
  556.8 2.3 copy-start.3
  559.0 2.7 copy-start.2
  567.1 2.0 copy-start.4
  572.0 2.0 copy-start.5
  578.1 2.3 copy-start.3
  580.3 2.7 copy-start.2
  588.4 2.0 copy-start.4
  593.3 2.0 copy-start.5
  599.3 2.3 copy-start.3
  638.6 32.9 %copy-start.1 = (bf16[64,64]{1,0:T(8,128)(2,1)S(1)}, bf16[64,64]{1,0:T(8,128)(2,1)}, u32[]{:S(2)}) copy-start(bf16[64,64]{1,0:T(8,128)(2,1)} %param.22) | copy-start | bytes 24580
  639.9 28.3 %collective-permute-start.4 = (bf16[4,64,1024]{2,1,0:T(8,128)(2,1)}, bf16[4,64,1024]{2,1,0:T(8,128)(2,1)}, u32[]{:S(2)}, u32[]{:S(2)}) collective-permute-start(bf16[4,64,1024]{2,1,0:T(8,128)(2,1)} %get-tuple-element.256), channel_id=1, source_target_pairs={{0,4},{4,8},{8,12},{12,16},{16,20},{20,24},{24,28},{1,5},{5,9},{9,... | collective-permute-start | bytes 1572872 | tf_op jit(solution)/shard_map/ppermute | solution.py:35
  641.8 26.4 %collective-permute-start.5 = (bf16[4,64,1024]{2,1,0:T(8,128)(2,1)}, bf16[4,64,1024]{2,1,0:T(8,128)(2,1)}, u32[]{:S(2)}, u32[]{:S(2)}) collective-permute-start(bf16[4,64,1024]{2,1,0:T(8,128)(2,1)} %get-tuple-element.257), channel_id=1, source_target_pairs={{4,0},{8,4},{12,8},{16,12},{20,16},{24,20},{28,24},{5,1},{9,5},{13... | collective-permute-start | bytes 1572872 | tf_op jit(solution)/shard_map/ppermute | solution.py:35
  646.1 18.4 %collective-permute-start.6 = (bf16[1024]{0:T(1024)(128)(2,1)S(1)}, bf16[1024]{0:T(1024)(128)(2,1)S(1)}, u32[]{:S(2)}, u32[]{:S(2)}) collective-permute-start(bf16[1024]{0:T(1024)(128)(2,1)S(1)} %get-tuple-element.258), channel_id=1, source_target_pairs={{0,4},{4,8},{8,12},{12,16},{16,20},{20,24},{24,28},{1,5},{5,9},{9,... | collective-permute-start | bytes 6152 | tf_op jit(solution)/shard_map/ppermute | solution.py:35
  648.0 20.1 %collective-permute-start.7 = (bf16[1024]{0:T(1024)(128)(2,1)S(1)}, bf16[1024]{0:T(1024)(128)(2,1)S(1)}, u32[]{:S(2)}, u32[]{:S(2)}) collective-permute-start(bf16[1024]{0:T(1024)(128)(2,1)S(1)} %get-tuple-element.259), channel_id=1, source_target_pairs={{4,0},{8,4},{12,8},{16,12},{20,16},{24,20},{28,24},{5,1},{9,5},{13... | collective-permute-start | bytes 6152 | tf_op jit(solution)/shard_map/ppermute | solution.py:35
Sparse Core Ops, SparseCore 0:
  8.9 59.8 all-gather.1
where the time goes:
time: 680 us; the launch traced here: 678 us
  waiting for transfers between devices  444 us (65%)
  other arithmetic  95.8 us (14%)
  local copies, waits for them, and re-layouts  44.6 us (7%)
  starting transfers between devices  25.8 us (4%)
  loops' own time  25.2 us (4%)
  matrix products  24.8 us (4%)
  between operations  18.3 us (3%)
    ppermute x2, waiting for transfers between devices, with_halo(): lax.ppermute(lax.slice_in_dim(block, block.shape[dim] - width, None, axis...  368 us
    all_gather x1, waiting for transfers between devices, body(): all_channels = lax.all_gather(features, 'member', axis=0, tiled=True)  61.6 us
    while x108, other arithmetic  27.5 us
    dot_general x24, matrix products, conv_same(): return jnp.dot(weight, stacked, preferred_element_type=jnp.float32)  24.6 us
    concatenate x2, other arithmetic, with_halo(): block = jnp.concatenate([low, block, high], axis=dim)  17.7 us
  transfers between devices with their start and end apart: 9, of which 5 were waited for; matrix products, arithmetic and copies ran while one was open for 1% of the time, Pallas kernels for 0%

commit v1 on v0

--- a/solution.py
+++ b/solution.py
@@ -125,7 +125,18 @@
     rim_width = REACH * tile_width
     ext_width = tile_width + 2 * rim_width
     tile_index = lax.axis_index("tile")
-    all_channels = lax.all_gather(features, "member", axis=0, tiled=True)
+    ways = lax.axis_size("member")
+    up = [(d, (d + 1) % ways) for d in range(ways)]
+    down = [(d, (d - 1) % ways) for d in range(ways)]
+    earlier_2, later = ([features], [features])
+    for _ in range(ways // 2):
+        earlier_2.append(lax.ppermute(earlier_2[-1], "member", up))
+    for _ in range((ways - 1) // 2):
+        later.append(lax.ppermute(later[-1], "member", down))
+    line = jnp.concatenate([*earlier_2[::-1], *later[1:]], axis=0)
+    all_channels = jnp.roll(
+        line, (lax.axis_index("member") - ways // 2) * features.shape[0], axis=0
+    )
     driver_ext = with_halo(all_channels, (("tile", 2),), rim_width)
     latent_ext = with_halo(latent[0].astype(jnp.bfloat16), (("tile", 2),), rim_width)
     current, earlier, sigma_sq = plan_terms(timestep)

time: 680 us -> 707 us (1.040)
  local copies, waits for them, and re-layouts: 44.6 us -> 75.2 us
  between operations: 18.3 us -> 4.99 us
  waiting for transfers between devices: 444 us -> 453 us
    ppermute x0 -> x3, waiting for transfers between devices: none -> 68.3 us  [the longest x2 68.3 us: body(): earlier_2.append(lax.ppermute(earlier_2[-1], 'member', up))]
    all_gather x1 -> x0, waiting for transfers between devices: 61.6 us -> none  [body(): all_channels = lax.all_gather(features, 'member', axis=0, tiled=True)]
    unnamed x14 -> x27, local copies, waits for them, and re-layouts: 0.04 us -> 19 us
    dynamic_slice x0 -> x1, local copies, waits for them, and re-layouts: none -> 8.48 us  [body(): jnp.roll(line, (lax.axis_index('member') - ways // 2) * features.shape[0]...]
  transfers between devices with their start and end apart: 9 -> 11, of which waited for: 5 -> 5; matrix products, arithmetic and copies ran while one was open for 1% -> 1% of each run, Pallas kernels for 0% -> 0%
where the time goes in v1:
time: 707 us; the launch traced here: 706 us
  waiting for transfers between devices  453 us (64%)
  other arithmetic  93.3 us (13%)
  local copies, waits for them, and re-layouts  75.2 us (11%)
  starting transfers between devices  29.1 us (4%)
  loops' own time  25.4 us (4%)
  matrix products  24.7 us (3%)
    ppermute x2, waiting for transfers between devices, with_halo(): lax.ppermute(lax.slice_in_dim(block, block.shape[dim] - width, None, axis...  370 us
    ppermute x2, waiting for transfers between devices, body(): earlier_2.append(lax.ppermute(earlier_2[-1], 'member', up))  68.3 us
    while x108, other arithmetic  27.5 us
    dot_general x24, matrix products, conv_same(): return jnp.dot(weight, stacked, preferred_element_type=jnp.float32)  24.5 us
    unnamed x27, local copies, waits for them, and re-layouts  19 us
    concatenate x2, other arithmetic, with_halo(): block = jnp.concatenate([low, block, high], axis=dim)  17.7 us
  transfers between devices with their start and end apart: 11, of which 5 were waited for; matrix products, arithmetic and copies ran while one was open for 1% of the time, Pallas kernels for 0%

profile of v1, /device:TPU:9, one launch (start us, length us, event | category | flops | bytes accessed | tf_op | source)
XLA Modules:
  0.0 705.9 jit_solution(10257742721989275901)
XLA Ops:
  0.0 1.8 collective-permute-start.2
  1.8 23.3 %collective-permute-done.2 = bf16[16,64,1024]{2,1,0:T(8,128)(2,1)} collective-permute-done((bf16[16,64,1024]{2,1,0:T(8,128)(2,1)}, bf16[16,64,1024]{2,1,0:T(8,128)(2,1)}, u32[]{:S(2)}, u32[]{:S(2)}) %collective-permute-start.2) | collective-permute-done | bytes 2097184 | tf_op jit(solution)/shard_map/ppermute | solution.py:133
  25.1 2.5 collective-permute-start.3
  27.6 45.0 %collective-permute-done.3 = bf16[16,64,1024]{2,1,0:T(8,128)(2,1)} collective-permute-done((bf16[16,64,1024]{2,1,0:T(8,128)(2,1)}, bf16[16,64,1024]{2,1,0:T(8,128)(2,1)}, u32[]{:S(2)}, u32[]{:S(2)}) %collective-permute-start.3) | collective-permute-done | bytes 2097184 | tf_op jit(solution)/shard_map/ppermute | solution.py:133
  72.5 3.2 constant_dynamic-update-slice_fusion.10
  75.7 3.1 constant_dynamic-update-slice_fusion.9
  78.8 1.6 constant_dynamic-update-slice_fusion.8
  80.4 3.2 constant_dynamic-update-slice_fusion.7
  83.5 3.2 constant_dynamic-update-slice_fusion.6
  86.8 3.1 constant_dynamic-update-slice_fusion.5
  89.9 1.6 constant_dynamic-update-slice_fusion.4
  91.5 3.2 constant_dynamic-update-slice_fusion.3
  94.6 8.5 %constant_dynamic-slice_fusion.1 = bf16[64,64,1024]{2,1,0:T(8,128)(2,1)} fusion(bf16[128,64,1024]{2,1,0:T(8,128)(2,1)} %constant_dynamic-update-slice_fusion.3, s32[]{:T(128)S(6)} %select_n.248), kind=kLoop, calls=%fused_computation.116 | loop fusion | bytes 16777220 | tf_op jit(solution)/shard_map/jit(_roll_dynamic)/dynamic_slice | solution.py:137
  103.1 3.1 collective-permute-start.5
  106.3 3.0 collective-permute-start.6
  109.4 2.2 collective-permute-start
  111.6 5.0 collective-permute-start.1
  117.7 370.5 %collective-permute-done = bf16[4,64,1024]{2,1,0:T(8,128)(2,1)S(1)} collective-permute-done((bf16[4,64,1024]{2,1,0:T(8,128)(2,1)S(1)}, bf16[4,64,1024]{2,1,0:T(8,128)(2,1)S(1)}, u32[]{:S(2)}, u32[]{:S(2)}) %collective-permute-start) | collective-permute-done | bytes 524320 | tf_op jit(solution)/shard_map/ppermute | solution.py:24
  488.2 2.5 collective-permute-done.1
  490.9 17.6 %pad_maximum_fusion = bf16[64,64,3072]{2,1,0:T(8,128)(2,1)} fusion(bf16[64,64,1024]{2,1,0:T(8,128)(2,1)} %collective-permute-done.6, bf16[64,64,1024]{2,1,0:T(8,128)(2,1)} %constant_dynamic-slice_fusion.1, bf16[64,64,1024]{2,1,0:T(8,128)(2,1)} %collective-permute-done.5), kind=kLoop, calls=%fused_computation.70 | loop fusion | flops 75497472 | bytes 50331648 | tf_op jit(solution)/shard_map/concatenate | solution.py:28
  508.5 127.5 %while.22 = (s32[]{:T(128)}, f32[6,4,4096]{2,1,0:T(4,128)}, s32[6]{0:T(128)S(1)}, bf16[4,64,3072]{2,1,0:T(8,128)(2,1)S(1)}, bf16[64,36]{0,1:T(8,128)(2,1)S(1)}, ...) while((s32[]{:T(128)}, f32[6,4,4096]{2,1,0:T(4,128)}, ...), condition=%wide.region_15.16_spmd, body=%wide.region_2.15_spmd.sunk | while | flops 663355456 | bytes 75635800 | solution.py:167
  511.9 1.6 dynamic-slice_convert_fusion.2
  518.4 1.1 fusion.64
  523.4 1.1 fusion.66
  528.3 1.4 fusion.67
  532.8 2.0 dynamic-slice_convert_fusion.2
  539.7 1.1 fusion.64
  544.6 1.1 fusion.66
  549.6 1.4 fusion.67
  554.1 2.0 dynamic-slice_convert_fusion.2
  561.0 1.1 fusion.64
  565.9 1.1 fusion.66
  570.8 1.4 fusion.67
  575.4 2.0 dynamic-slice_convert_fusion.2
  582.2 1.1 fusion.64
  587.2 1.1 fusion.66
  592.1 1.4 fusion.67
  596.6 2.0 dynamic-slice_convert_fusion.2
  603.5 1.1 fusion.64
  608.5 1.1 fusion.66
  613.4 1.4 fusion.67
  617.9 2.0 dynamic-slice_convert_fusion.2
  624.8 1.1 fusion.64
  629.7 1.1 fusion.66
  634.6 1.4 fusion.67
  636.4 36.7 %while.23 = (s32[]{:T(128)}, f32[4,64,3072]{2,1,0:T(8,128)S(1)}, s32[6]{0:T(128)S(1)}, f32[6]{0:T(128)S(1)}, f32[6,4,4096]{2,1,0:T(4,128)}, /*index=5*/s32[]{:T(128)}, s32[]{:T(128)}, s32[]{:T(128)}) while((s32[]{:T(128)}, f32[4,64,3072]{2,1,0:T(8,128)S(1)}, s32[6]{0:T(128)S(1)}, f32[6]{0:T(128)S(1)}, f32[6,4,4096]{2,1,0:T(4,128)}, ...), condition=%wide.region_17.18_spmd, body=%wide.region_16.17_spmd.sunk | while | flops 32773 | bytes 589983 | solution.py:175
  639.8 1.5 dynamic-slice_multiply_fusion.2
  641.6 1.0 dynamic_update_slice.14
  646.0 1.5 dynamic-slice_multiply_fusion.2
  651.7 1.5 dynamic-slice_multiply_fusion.2
  653.5 1.1 dynamic_update_slice.14
  658.0 1.5 dynamic-slice_multiply_fusion.2
  659.8 1.1 dynamic_update_slice.14
  664.4 1.5 dynamic-slice_multiply_fusion.2
  666.2 1.1 dynamic_update_slice.14
  670.7 1.5 dynamic-slice_multiply_fusion.2
  673.3 1.0 fusion.29
  674.3 1.9 collective-permute-start.7
  676.2 4.3 collective-permute-start.8
  680.5 1.9 collective-permute-start.10
  682.4 3.4 collective-permute-start.9
  685.8 0.8 select_reduce_fusion.1
  690.6 12.0 %collective-permute-done.10 = bf16[1024]{0:T(1024)(128)(2,1)S(1)} collective-permute-done((bf16[1024]{0:T(1024)(128)(2,1)S(1)}, bf16[1024]{0:T(1024)(128)(2,1)S(1)}, u32[]{:S(2)}, u32[]{:S(2)}) %collective-permute-start.10) | collective-permute-done | bytes 2080 | tf_op jit(solution)/shard_map/ppermute | solution.py:35
  702.6 3.3 fusion.12
  (541 shorter events, 92.8 us)
Async XLA Ops:
  0.0 117.5 %copy-start = (bf16[64,64]{1,0:T(8,128)(2,1)S(1)}, bf16[64,64]{1,0:T(8,128)(2,1)}, u32[]{:S(2)}) copy-start(bf16[64,64]{1,0:T(8,128)(2,1)} %param.22) | copy-start | bytes 24580
  0.0 78.8 %copy-start.2 = (bf16[16,64,1024]{2,1,0:T(8,128)(2,1)S(1)}, bf16[16,64,1024]{2,1,0:T(8,128)(2,1)}, u32[]{:S(2)}) copy-start(bf16[16,64,1024]{2,1,0:T(8,128)(2,1)} %param.19) | copy-start | bytes 6291460
  0.0 25.1 %collective-permute-start.2 = (bf16[16,64,1024]{2,1,0:T(8,128)(2,1)}, bf16[16,64,1024]{2,1,0:T(8,128)(2,1)}, u32[]{:S(2)}, u32[]{:S(2)}) collective-permute-start(bf16[16,64,1024]{2,1,0:T(8,128)(2,1)} %param.19), channel_id=1, source_target_pairs={{0,1},{1,2},{2,3},{3,0},{4,5},{5,6},{6,7},{7,4},{8,9},{9,10},{10,1... | collective-permute-start | bytes 6291464 | tf_op jit(solution)/shard_map/ppermute | solution.py:133
  25.1 47.4 %collective-permute-start.3 = (bf16[16,64,1024]{2,1,0:T(8,128)(2,1)}, bf16[16,64,1024]{2,1,0:T(8,128)(2,1)}, u32[]{:S(2)}, u32[]{:S(2)}) collective-permute-start(bf16[16,64,1024]{2,1,0:T(8,128)(2,1)} %collective-permute-done.2), channel_id=1, source_target_pairs={{0,1},{1,2},{2,3},{3,0},{4,5},{5,6},{6,7},{7,4},{8,9},{9,10},{10,1... | collective-permute-start | bytes 6291464 | tf_op jit(solution)/shard_map/ppermute | solution.py:133
  27.6 52.8 %collective-permute-start.4 = (bf16[16,64,1024]{2,1,0:T(8,128)(2,1)}, bf16[16,64,1024]{2,1,0:T(8,128)(2,1)}, u32[]{:S(2)}, u32[]{:S(2)}) collective-permute-start(bf16[16,64,1024]{2,1,0:T(8,128)(2,1)} %param.19), channel_id=1, source_target_pairs={{0,3},{1,0},{2,1},{3,2},{4,7},{5,4},{6,5},{7,6},{8,11},{9,8},{10,9... | collective-permute-start | bytes 6291464 | tf_op jit(solution)/shard_map/ppermute | solution.py:135
  94.6 14.7 %copy-start.3 = (f32[1,4,64,1024]{3,2,1,0:T(8,128)S(1)}, f32[1,4,64,1024]{3,2,1,0:T(8,128)}, u32[]{:S(2)}) copy-start(f32[1,4,64,1024]{3,2,1,0:T(8,128)} %param.17) | copy-start | bytes 3145732
  94.6 22.0 %copy-start.13 = (s32[6]{0:T(128)S(1)}, s32[6]{0:T(128)}, u32[]{:S(2)}) copy-start(s32[6]{0:T(128)} %param.20) | copy-start | bytes 76
  103.1 387.8 %collective-permute-start.5 = (bf16[64,64,1024]{2,1,0:T(8,128)(2,1)}, bf16[64,64,1024]{2,1,0:T(8,128)(2,1)}, u32[]{:S(2)}, u32[]{:S(2)}) collective-permute-start(bf16[64,64,1024]{2,1,0:T(8,128)(2,1)} %constant_dynamic-slice_fusion.1), channel_id=1, source_target_pairs={{0,4},{4,8},{8,12},{12,16},{16,20},{20,24},{24,28},{1,5},{5,9},{9,... | collective-permute-start | bytes 25165832 | tf_op jit(solution)/shard_map/ppermute | solution.py:24
  106.3 384.6 %collective-permute-start.6 = (bf16[64,64,1024]{2,1,0:T(8,128)(2,1)}, bf16[64,64,1024]{2,1,0:T(8,128)(2,1)}, u32[]{:S(2)}, u32[]{:S(2)}) collective-permute-start(bf16[64,64,1024]{2,1,0:T(8,128)(2,1)} %constant_dynamic-slice_fusion.1), channel_id=1, source_target_pairs={{4,0},{8,4},{12,8},{16,12},{20,16},{24,20},{28,24},{5,1},{9,5},{13... | collective-permute-start | bytes 25165832 | tf_op jit(solution)/shard_map/ppermute | solution.py:27
  109.4 378.8 %collective-permute-start = (bf16[4,64,1024]{2,1,0:T(8,128)(2,1)S(1)}, bf16[4,64,1024]{2,1,0:T(8,128)(2,1)S(1)}, u32[]{:S(2)}, u32[]{:S(2)}) collective-permute-start(bf16[4,64,1024]{2,1,0:T(8,128)(2,1)S(1)} %bitcast_convert_fusion), channel_id=1, source_target_pairs={{0,4},{4,8},{8,12},{12,16},{16,20},{20,24},{24,28},{1,5},{5,9},{9,... | collective-permute-start | bytes 1572872 | tf_op jit(solution)/shard_map/ppermute | solution.py:24
  111.6 379.1 %collective-permute-start.1 = (bf16[4,64,1024]{2,1,0:T(8,128)(2,1)S(1)}, bf16[4,64,1024]{2,1,0:T(8,128)(2,1)S(1)}, u32[]{:S(2)}, u32[]{:S(2)}) collective-permute-start(bf16[4,64,1024]{2,1,0:T(8,128)(2,1)S(1)} %bitcast_convert_fusion), channel_id=1, source_target_pairs={{4,0},{8,4},{12,8},{16,12},{20,16},{24,20},{28,24},{5,1},{9,5},{13... | collective-permute-start | bytes 1572872 | tf_op jit(solution)/shard_map/ppermute | solution.py:27
  490.8 17.7 %copy-start.8 = (bf16[64,36]{0,1:T(8,128)(2,1)S(1)}, bf16[64,36]{0,1:T(8,128)(2,1)}, u32[]{:S(2)}) copy-start(bf16[64,36]{0,1:T(8,128)(2,1)} %param.23) | copy-start | bytes 13828
  490.8 17.7 %copy-start.9 = (bf16[4,576]{1,0:T(4,128)(2,1)S(1)}, bf16[4,576]{1,0:T(4,128)(2,1)}, u32[]{:S(2)}) copy-start(bf16[4,576]{1,0:T(4,128)(2,1)} %param.26) | copy-start | bytes 13828
  490.9 17.7 %copy-start.10 = (f32[64]{0:T(128)S(1)}, f32[64]{0:T(128)}, u32[]{:S(2)}) copy-start(f32[64]{0:T(128)} %param.27) | copy-start | bytes 772
  490.9 17.7 %copy-start.11 = (f32[64]{0:T(128)S(1)}, f32[64]{0:T(128)}, u32[]{:S(2)}) copy-start(f32[64]{0:T(128)} %param.28) | copy-start | bytes 772
  490.9 17.7 %copy-start.12 = (f32[64]{0:T(128)S(1)}, f32[64]{0:T(128)}, u32[]{:S(2)}) copy-start(f32[64]{0:T(128)} %param.29) | copy-start | bytes 772
  508.7 2.7 copy-start.4
  516.4 2.0 copy-start.6
  521.4 2.0 copy-start.7
  527.4 2.3 copy-start.5
  529.7 2.7 copy-start.4
  537.7 2.0 copy-start.6
  542.6 2.0 copy-start.7
  548.7 2.3 copy-start.5
  550.9 2.7 copy-start.4
  559.0 2.0 copy-start.6
  563.9 2.0 copy-start.7
  569.9 2.3 copy-start.5
  572.2 2.7 copy-start.4
  580.3 2.0 copy-start.6
  585.2 2.0 copy-start.7
  591.2 2.3 copy-start.5
  593.5 2.7 copy-start.4
  601.5 2.0 copy-start.6
  606.5 2.0 copy-start.7
  612.5 2.3 copy-start.5
  614.7 2.7 copy-start.4
  622.8 2.0 copy-start.6
  627.7 2.0 copy-start.7
  633.8 2.3 copy-start.5
  673.0 32.9 %copy-start.1 = (bf16[64,64]{1,0:T(8,128)(2,1)S(1)}, bf16[64,64]{1,0:T(8,128)(2,1)}, u32[]{:S(2)}) copy-start(bf16[64,64]{1,0:T(8,128)(2,1)} %param.22) | copy-start | bytes 24580
  674.3 28.3 %collective-permute-start.7 = (bf16[4,64,1024]{2,1,0:T(8,128)(2,1)}, bf16[4,64,1024]{2,1,0:T(8,128)(2,1)}, u32[]{:S(2)}, u32[]{:S(2)}) collective-permute-start(bf16[4,64,1024]{2,1,0:T(8,128)(2,1)} %get-tuple-element.256), channel_id=1, source_target_pairs={{0,4},{4,8},{8,12},{12,16},{16,20},{20,24},{24,28},{1,5},{5,9},{9,... | collective-permute-start | bytes 1572872 | tf_op jit(solution)/shard_map/ppermute | solution.py:35
  676.2 26.4 %collective-permute-start.8 = (bf16[4,64,1024]{2,1,0:T(8,128)(2,1)}, bf16[4,64,1024]{2,1,0:T(8,128)(2,1)}, u32[]{:S(2)}, u32[]{:S(2)}) collective-permute-start(bf16[4,64,1024]{2,1,0:T(8,128)(2,1)} %get-tuple-element.257), channel_id=1, source_target_pairs={{4,0},{8,4},{12,8},{16,12},{20,16},{24,20},{28,24},{5,1},{9,5},{13... | collective-permute-start | bytes 1572872 | tf_op jit(solution)/shard_map/ppermute | solution.py:35
  680.5 22.1 %collective-permute-start.10 = (bf16[1024]{0:T(1024)(128)(2,1)S(1)}, bf16[1024]{0:T(1024)(128)(2,1)S(1)}, u32[]{:S(2)}, u32[]{:S(2)}) collective-permute-start(bf16[1024]{0:T(1024)(128)(2,1)S(1)} %get-tuple-element.259), channel_id=1, source_target_pairs={{4,0},{8,4},{12,8},{16,12},{20,16},{24,20},{28,24},{5,1},{9,5},{13... | collective-permute-start | bytes 6152 | tf_op jit(solution)/shard_map/ppermute | solution.py:35
  682.4 20.1 %collective-permute-start.9 = (bf16[1024]{0:T(1024)(128)(2,1)S(1)}, bf16[1024]{0:T(1024)(128)(2,1)S(1)}, u32[]{:S(2)}, u32[]{:S(2)}) collective-permute-start(bf16[1024]{0:T(1024)(128)(2,1)S(1)} %get-tuple-element.258), channel_id=1, source_target_pairs={{0,4},{4,8},{8,12},{12,16},{16,20},{20,24},{24,28},{1,5},{5,9},{9,... | collective-permute-start | bytes 6152 | tf_op jit(solution)/shard_map/ppermute | solution.py:35
